TPU v7x, 1024 devices: a whole 4x8x16 slice. The times are simulated.
1024 devices in a mesh: gx: 16 (over z), gy: 8 (over x, core), band: 8 (over y).
Axes of the slice: x: 4, y: 8, z: 16, core: 2. Of those that a mesh axis runs over, the one named last changes fastest.
Arguments:
- orbitals: float32 [32, 128, 64, 128], P('band', 'gx', 'gy'), may hold values from -6 to 6
- potential: float32 [128, 64, 128], P('gx', 'gy'), may hold values from -2 to 1
Outputs:
- rotated: float32 [32, 128, 64, 128], P('band', 'gx', 'gy')
All inputs are finite; a program needn't handle non-finite values.
Results may differ from a plain program's by a relative error of at most 0.00007.
Values sent between devices are 32-bit elements; how exact they have to be, the bound alone decides.
A program may use at most 32 MiB of HBM per device.

v0:
```python
import jax
import jax.numpy as jnp
from jax import lax
from jax.sharding import PartitionSpec as P

COEF = (
    -5369.0 / 1800.0,
    12.0 / 7.0,
    -15.0 / 56.0,
    10.0 / 189.0,
    -1.0 / 112.0,
    2.0 / 1925.0,
    -1.0 / 16632.0,
)
LOWER_EDGE = 4.0
UPPER_EDGE = 16.0
BOTTOM_EDGE = -2.5


def with_halo(block, sides, width):
    for axis, dim in sides:
        count = lax.axis_size(axis)
        forward = [(i, i + 1) for i in range(count - 1)]
        forward.append((count - 1, 0))
        backward = [(target, source) for source, target in forward]
        low = lax.ppermute(
            lax.slice_in_dim(block, block.shape[dim] - width, None, axis=dim), axis, forward
        )
        high = lax.ppermute(lax.slice_in_dim(block, 0, width, axis=dim), axis, backward)
        block = jnp.concatenate([low, block, high], axis=dim)
    return block


def hamiltonian(field, potential):
    padded = with_halo(field, (("gx", 1), ("gy", 2)), 6)
    width_x = field.shape[1]
    width_y = field.shape[2]
    depth_z = field.shape[3]
    wrapped = jnp.concatenate([field[..., depth_z - 6 :], field, field[..., :6]], axis=3)
    laplace = 3.0 * COEF[0] * field
    for offset in range(1, 7):
        beside_all = padded[:, 6 + offset : 6 + offset + width_x, 6 : 6 + width_y, :]
        beside_all = beside_all + padded[:, 6 - offset : 6 - offset + width_x, 6 : 6 + width_y, :]
        beside_all = beside_all + padded[:, 6 : 6 + width_x, 6 + offset : 6 + offset + width_y, :]
        beside_all = beside_all + padded[:, 6 : 6 + width_x, 6 - offset : 6 - offset + width_y, :]
        beside_all = beside_all + wrapped[..., 6 + offset : 6 + offset + depth_z]
        beside_all = beside_all + wrapped[..., 6 - offset : 6 - offset + depth_z]
        laplace = laplace + COEF[offset] * beside_all
    return -0.5 * laplace + potential[None] * field


def local(orbitals, potential):
    half_width = (UPPER_EDGE - LOWER_EDGE) / 2.0
    centre = (UPPER_EDGE + LOWER_EDGE) / 2.0
    sigma_first = half_width / (BOTTOM_EDGE - centre)
    sigma_now = sigma_first
    earlier = orbitals
    current = (hamiltonian(orbitals, potential) - centre * orbitals) * (sigma_first / half_width)
    for order_index in range(2):
        sigma_next = 1.0 / (2.0 / sigma_first - sigma_now)
        latest = (
            2.0 * sigma_next / half_width * (hamiltonian(current, potential) - centre * current)
            - sigma_now * sigma_next * earlier
        )
        earlier = current
        current = latest
        sigma_now = sigma_next
    local_bands = current.shape[0]
    flat = current.reshape(local_bands, -1)
    cells_all = float(flat.shape[1] * lax.axis_size("gx") * lax.axis_size("gy"))
    total_bands = local_bands * lax.axis_size("band")
    identity = jnp.eye(total_bands, dtype=jnp.float32)
    every = lax.all_gather(flat, "band", axis=0, tiled=True)
    partial_sum = jnp.dot(
        every, every.T, precision=lax.Precision.HIGHEST, preferred_element_type=jnp.float32
    )
    intersection = lax.psum(partial_sum, ("gx", "gy")) / cells_all
    lower = jnp.linalg.cholesky(intersection)
    inverse = lax.linalg.triangular_solve(lower, identity, left_side=True, lower=True)
    my_rows = lax.dynamic_slice_in_dim(
        inverse, lax.axis_index("band") * local_bands, local_bands, 0
    )
    result = jnp.dot(
        my_rows, every, precision=lax.Precision.HIGHEST, preferred_element_type=jnp.float32
    )
    return result.reshape(current.shape)


def solution(mesh):
    in_specs = (P("band", "gx", "gy", None), P("gx", "gy", None))
    out_specs = P("band", "gx", "gy", None)
    return jax.shard_map(local, mesh=mesh, in_specs=in_specs, out_specs=out_specs, check_vma=False)
```

profile of v0, /device:TPU:1, one launch (start us, length us, event | category | flops | bytes accessed | tf_op | source)
XLA Modules:
  0.0 626.7 jit_solution(11155328406234377022)
XLA Ops:
  6.5 1.0 fusion.203
  7.5 4.8 collective-permute-start.1
  12.4 16.0 %collective-permute-start = (f32[4,6,8,128]{3,2,1,0:T(8,128)S(1)}, f32[4,6,8,128]{3,2,1,0:T(8,128)S(1)}, u32[]{:S(2)}, u32[]{:S(2)}) collective-permute-start(f32[4,6,8,128]{3,2,1,0:T(8,128)S(1)} %get-tuple-element.28), channel_id=1, source_target_pairs={{64,0},{128,64},{192,128},{256,192},{320,256},{384,320},{448,384},... | collective-permute-start | bytes 294920 | tf_op jit(solution)/shard_map/ppermute | solution.py:29
  28.9 1.1 collective-permute-done
  30.1 1.5 collective-permute-start.2
  31.6 1.1 collective-permute-start.3
  32.8 4.9 collective-permute-done.2
  38.6 5.2 collective-permute-start.4
  43.9 1.9 collective-permute-start.5
  45.8 4.6 collective-permute-done.5
  50.5 4.0 collective-permute-start.6
  54.7 3.8 collective-permute-done.6
  58.7 0.9 fusion.64
  59.6 1.9 collective-permute-start.8
  61.5 3.4 collective-permute-start.9
  65.0 3.1 collective-permute-done.9
  68.2 4.9 collective-permute-start.10
  73.2 3.4 collective-permute-done.10
  78.8 36.6 %all-gather.3.cloned.1.call-done = f32[8,4,8192]{2,1,0:T(4,128)} async-done(((f32[1,4,8192]{2,1,0:T(4,128)}), f32[8,4,8192]{2,1,0:T(4,128)}) %all-gather.3.cloned.1.call-update) | async-done | bytes 1048592 | tf_op jit(solution)/shard_map/all_gather | solution.py:73
  115.4 1.6 reshape.19
  117.0 1.0 fusion.205
  117.9 493.7 %psum.7 = f32[32,32]{0,1:T(8,128)S(1)} all-reduce(f32[32,32]{0,1:T(8,128)S(1)} %fusion.205), channel_id=1, replica_groups=mesh['gx'=16,'gy'=8,'band'=8] {'gx','gy'}, use_global_device_ids=true, to_apply=%region_0.0 | all-reduce | flops 1024 | bytes 8192 | tf_op jit(solution)/shard_map/psum | solution.py:77
  611.7 2.9 cholesky.17
  615.9 2.4 custom-call.6
  (42 shorter events, 7.3 us)
Async XLA Ops:
  6.5 108.9 %all-gather.3.cloned.1.call-start = ((), (), s32[]{:S(2)}) async-start(), calls=%async_computation | async-start | bytes 1179648 | tf_op jit(solution)/shard_map/all_gather | solution.py:73
  7.5 21.3 %collective-permute-start.1 = (f32[4,6,8,128]{3,2,1,0:T(8,128)S(1)}, f32[4,6,8,128]{3,2,1,0:T(8,128)S(1)}, u32[]{:S(2)}, u32[]{:S(2)}) collective-permute-start(f32[4,6,8,128]{3,2,1,0:T(8,128)S(1)} %get-tuple-element.29), channel_id=1, source_target_pairs={{0,64},{64,128},{128,192},{192,256},{256,320},{320,384},{384,448},... | collective-permute-start | bytes 294920 | tf_op jit(solution)/shard_map/ppermute | solution.py:26
  12.4 16.5 %copy-start = (f32[4,8,8,128]{3,2,1,0:T(8,128)S(1)}, f32[4,8,8,128]{3,2,1,0:T(8,128)}, u32[]{:S(2)}) copy-start(f32[4,8,8,128]{3,2,1,0:T(8,128)} %param.2) | copy-start | bytes 393220
  12.4 17.6 %collective-permute-start = (f32[4,6,8,128]{3,2,1,0:T(8,128)S(1)}, f32[4,6,8,128]{3,2,1,0:T(8,128)S(1)}, u32[]{:S(2)}, u32[]{:S(2)}) collective-permute-start(f32[4,6,8,128]{3,2,1,0:T(8,128)S(1)} %get-tuple-element.28), channel_id=1, source_target_pairs={{64,0},{128,64},{192,128},{256,192},{320,256},{384,320},{448,384},... | collective-permute-start | bytes 294920 | tf_op jit(solution)/shard_map/ppermute | solution.py:29
  30.1 7.7 %collective-permute-start.2 = (f32[4,20,6,128]{3,2,1,0:T(8,128)S(1)}, f32[4,20,6,128]{3,2,1,0:T(8,128)S(1)}, u32[]{:S(2)}, u32[]{:S(2)}) collective-permute-start(f32[4,20,6,128]{3,2,1,0:T(8,128)S(1)} %get-tuple-element.15), channel_id=1, source_target_pairs={{8,0},{16,8},{24,16},{32,24},{40,32},{48,40},{56,48},{0,56},{9,1},... | collective-permute-start | bytes 737288 | tf_op jit(solution)/shard_map/ppermute | solution.py:29
  31.6 6.2 copy-start.1
  31.6 6.2 collective-permute-start.3
  38.6 7.2 %collective-permute-start.4 = (f32[4,6,8,128]{3,2,1,0:T(8,128)S(1)}, f32[4,6,8,128]{3,2,1,0:T(8,128)S(1)}, u32[]{:S(2)}, u32[]{:S(2)}) collective-permute-start(f32[4,6,8,128]{3,2,1,0:T(8,128)S(1)} %get-tuple-element.23), channel_id=1, source_target_pairs={{64,0},{128,64},{192,128},{256,192},{320,256},{384,320},{448,384},... | collective-permute-start | bytes 294920 | tf_op jit(solution)/shard_map/ppermute | solution.py:29
  43.9 6.6 %collective-permute-start.5 = (f32[4,6,8,128]{3,2,1,0:T(8,128)S(1)}, f32[4,6,8,128]{3,2,1,0:T(8,128)S(1)}, u32[]{:S(2)}, u32[]{:S(2)}) collective-permute-start(f32[4,6,8,128]{3,2,1,0:T(8,128)S(1)} %get-tuple-element.24), channel_id=1, source_target_pairs={{0,64},{64,128},{128,192},{192,256},{256,320},{320,384},{384,448},... | collective-permute-start | bytes 294920 | tf_op jit(solution)/shard_map/ppermute | solution.py:26
  50.5 8.0 %collective-permute-start.6 = (f32[4,20,6,128]{3,2,1,0:T(8,128)S(1)}, f32[4,20,6,128]{3,2,1,0:T(8,128)S(1)}, u32[]{:S(2)}, u32[]{:S(2)}) collective-permute-start(f32[4,20,6,128]{3,2,1,0:T(8,128)S(1)} %get-tuple-element.13), channel_id=1, source_target_pairs={{8,0},{16,8},{24,16},{32,24},{40,32},{48,40},{56,48},{0,56},{9,1},... | collective-permute-start | bytes 737288 | tf_op jit(solution)/shard_map/ppermute | solution.py:29
  54.6 4.0 collective-permute-start.7
  59.6 5.4 collective-permute-start.8
  61.5 6.6 %collective-permute-start.9 = (f32[4,6,8,128]{3,2,1,0:T(8,128)S(1)}, f32[4,6,8,128]{3,2,1,0:T(8,128)S(1)}, u32[]{:S(2)}, u32[]{:S(2)}) collective-permute-start(f32[4,6,8,128]{3,2,1,0:T(8,128)S(1)} %get-tuple-element.20), channel_id=1, source_target_pairs={{0,64},{64,128},{128,192},{192,256},{256,320},{320,384},{384,448},... | collective-permute-start | bytes 294920 | tf_op jit(solution)/shard_map/ppermute | solution.py:26
  68.2 8.4 %collective-permute-start.10 = (f32[4,20,6,128]{3,2,1,0:T(8,128)S(1)}, f32[4,20,6,128]{3,2,1,0:T(8,128)S(1)}, u32[]{:S(2)}, u32[]{:S(2)}) collective-permute-start(f32[4,20,6,128]{3,2,1,0:T(8,128)S(1)} %get-tuple-element.9), channel_id=1, source_target_pairs={{8,0},{16,8},{24,16},{32,24},{40,32},{48,40},{56,48},{0,56},{9,1},... | collective-permute-start | bytes 737288 | tf_op jit(solution)/shard_map/ppermute | solution.py:29
  73.1 4.0 collective-permute-start.11
Sparse Core Ops, SparseCore 0:
  78.9 36.4 all-gather.2
where the time goes:
time: 630 us; the launch traced here: 627 us
  blocking collectives  494 us (78%)
  waiting for transfers between devices  58.7 us (9%)
  starting transfers between devices  44.9 us (7%)
  between operations  13.6 us (2%)
  other arithmetic  9.55 us (2%)
    psum x1, blocking collectives, local(): intersection = lax.psum(partial_sum, ('gx', 'gy')) / cells_all  494 us
    all_gather x1, waiting for transfers between devices, local(): every = lax.all_gather(flat, 'band', axis=0, tiled=True)  36.6 us
    ppermute x6, starting transfers between devices, with_halo(): lax.ppermute(lax.slice_in_dim(block, 0, width, axis=dim), axis, backward)  33.6 us
    ppermute x6, waiting for transfers between devices, with_halo(): lax.ppermute(lax.slice_in_dim(block, 0, width, axis=dim), axis, backward)  13.4 us
  transfers between devices with their start and end apart: 13, of which 11 were waited for; matrix products, arithmetic and copies ran while one was open for 0% of the time, Pallas kernels for 0%

commit v1 on v0

v1 whole, which is shorter than its diff:
```python
import functools

import jax
import jax.numpy as jnp
from jax import lax
from jax.experimental import pallas as pl
from jax.experimental.pallas import tpu as pltpu
from jax.sharding import PartitionSpec as P

COEF = (
    -5369.0 / 1800.0,
    12.0 / 7.0,
    -15.0 / 56.0,
    10.0 / 189.0,
    -1.0 / 112.0,
    2.0 / 1925.0,
    -1.0 / 16632.0,
)
LOWER_EDGE = 4.0
UPPER_EDGE = 16.0
BOTTOM_EDGE = -2.5
REACH = 6
MESH = pl.DeviceIdType.MESH


def chebyshev_weights():
    half = (UPPER_EDGE - LOWER_EDGE) / 2.0
    centre = (UPPER_EDGE + LOWER_EDGE) / 2.0
    first = half / (BOTTOM_EDGE - centre)
    rounds = [(first / half, 0.0)]
    now = first
    for _ in range(2):
        following = 1.0 / (2.0 / first - now)
        rounds.append((2.0 * following / half, now * following))
        now = following
    return centre, rounds


CENTRE, ROUNDS = chebyshev_weights()


def split_three(value):
    high = value.astype(jnp.bfloat16)
    rest = value - high.astype(jnp.float32)
    middle = rest.astype(jnp.bfloat16)
    low = (rest - middle.astype(jnp.float32)).astype(jnp.bfloat16)
    return high, middle, low


def kernel(
    sizes, orb_ref, pot_ref, out_ref, xb, yb, acc, fown, fc, rb, ob, sums_gy, sums_band, sums_gx, gram,
    load_sem, x_send, x_recv, y_send, y_recv, a_send, a_recv, b_send, b_recv,
    gy_send, gy_recv, band_send, band_recv, gx_send, gx_recv,
):
    n_gx, n_gy, n_band = sizes
    n_orb, n_x, n_y, n_z = out_ref.shape
    total = n_orb * n_band
    gx = lax.axis_index("gx")
    gy = lax.axis_index("gy")
    band = lax.axis_index("band")
    me = {"gx": gx, "gy": gy, "band": band}
    counts = {"gx": n_gx, "gy": n_gy, "band": n_band}

    def peer(axis, step):
        return lax.rem(me[axis] + step, counts[axis])

    barrier = pltpu.get_barrier_semaphore()
    for axis in ("gx", "gy", "band"):
        @pl.loop(1, counts[axis])
        def _(step, axis=axis):
            pl.semaphore_signal(
                barrier, inc=1, device_id={axis: peer(axis, step)}, device_id_type=MESH
            )

    own_x = pl.ds(REACH, n_x)
    own_y = pl.ds(n_y, n_y)
    load_x = pltpu.make_async_copy(orb_ref, xb.at[0, :, own_x], load_sem.at[0])
    load_y = pltpu.make_async_copy(orb_ref, yb.at[0, :, :, own_y], load_sem.at[1])
    load_x.start()
    load_y.start()
    load_x.wait()
    load_y.wait()
    pl.semaphore_wait(barrier, n_gx + n_gy + n_band - 3)

    def halo(r, o):
        right_x = {"gx": peer("gx", 1)}
        left_x = {"gx": peer("gx", n_gx - 1)}
        right_y = {"gy": peer("gy", 1)}
        left_y = {"gy": peer("gy", n_gy - 1)}

        def move(buf, src, dst, send, recv, target):
            return pltpu.make_async_remote_copy(
                src_ref=buf.at[src], dst_ref=buf.at[dst], send_sem=send, recv_sem=recv,
                device_id=target, device_id_type=MESH,
            )

        every = slice(None)
        return (
            move(xb, (r, o, pl.ds(n_x, REACH)), (r, o, pl.ds(0, REACH)),
                 x_send.at[r, 0, o], x_recv.at[r, 0, o], right_x),
            move(xb, (r, o, pl.ds(REACH, REACH)), (r, o, pl.ds(n_x + REACH, REACH)),
                 x_send.at[r, 1, o], x_recv.at[r, 1, o], left_x),
            move(yb, (r, o, every, pl.ds(2 * n_y - REACH, REACH)),
                 (r, o, every, pl.ds(n_y - REACH, REACH)),
                 y_send.at[r, 0, o], y_recv.at[r, 0, o], right_y),
            move(yb, (r, o, every, pl.ds(n_y, REACH)), (r, o, every, pl.ds(2 * n_y, REACH)),
                 y_send.at[r, 1, o], y_recv.at[r, 1, o], left_y),
        )

    def local_part(r, o):
        scale, back = ROUNDS[r]
        value = xb[r, o, own_x]
        result = scale * ((pot_ref[...] - (1.5 * COEF[0] + CENTRE)) * value)
        if r > 0:
            result = result - back * xb[r - 1, o, own_x]
        flat = value.reshape(n_x * n_y, n_z)
        along_z = jnp.zeros_like(flat)
        for k in range(1, REACH + 1):
            pair = pltpu.roll(flat, k, 1) + pltpu.roll(flat, n_z - k, 1)
            along_z = along_z + (-0.5 * COEF[k] * scale) * pair
        acc[o] = result + along_z.reshape(n_x, n_y, n_z)

    def halo_part(r, o):
        scale = ROUNDS[r][0]
        result = acc[o]
        for k in range(1, REACH + 1):
            pair = xb[r, o, pl.ds(REACH + k, n_x)] + xb[r, o, pl.ds(REACH - k, n_x)]
            pair = pair + yb[r, o, :, pl.ds(n_y + k, n_y)]
            pair = pair + yb[r, o, :, pl.ds(n_y - k, n_y)]
            result = result + (-0.5 * COEF[k] * scale) * pair
        return result

    @pl.loop(0, n_orb)
    def _(o):
        for copy in halo(0, o):
            copy.start()

    @pl.loop(0, n_orb)
    def _(o):
        local_part(0, o)

    for r in range(3):
        @pl.loop(0, n_orb)
        def _(o, r=r):
            for copy in halo(r, o):
                copy.wait_recv()
            result = halo_part(r, o)
            if r < 2:
                xb[r + 1, o, own_x] = result
                yb[r + 1, o, :, own_y] = result
                for copy in halo(r + 1, o):
                    copy.start()
                local_part(r + 1, o)
            else:
                fown[:, pl.ds(pl.multiple_of(o * n_y, n_y), n_y)] = result

    depth = n_orb * n_y

    def rows_of(index):
        return pl.ds(pl.multiple_of(depth * index, depth), depth)

    def spread(source, target):
        return pltpu.make_async_remote_copy(
            src_ref=fown.at[target], dst_ref=fc.at[rows_of(source)],
            send_sem=a_send.at[target], recv_sem=a_recv.at[source],
            device_id={"band": target}, device_id_type=MESH,
        )

    @pl.loop(1, n_band)
    def _(step):
        spread(band, peer("band", step)).start()

    fc[rows_of(band)] = fown[band]

    @pl.loop(1, n_band)
    def _(step):
        spread(peer("band", step), peer("band", step)).wait_recv()

    parts = []
    for y in range(n_y):
        parts.append(split_three(fc[pl.ds(y, total, stride=n_y), :]))
    stacked = jnp.concatenate([jnp.concatenate(part, axis=0) for part in parts], axis=1)
    blocks = lax.dot_general(
        stacked, stacked, (((1,), (1,)), ((), ())), preferred_element_type=jnp.float32
    )
    blocks = blocks[:total] + blocks[total : 2 * total] + blocks[2 * total :]
    gram[:, : 3 * total] = blocks
    gram[:, 3 * total :] = jnp.zeros((total, n_z - 3 * total), jnp.float32)
    wide = gram[...]
    wide = wide + pltpu.roll(wide, n_z - total, 1) + pltpu.roll(wide, n_z - 2 * total, 1)
    lane = lax.broadcasted_iota(jnp.int32, (8, n_z), 1)
    row = lax.broadcasted_iota(jnp.int32, (8, n_z), 0)
    groups = total // 8
    packed = jnp.where(lane < total, wide[:8], 0.0)
    for q in range(1, groups):
        moved = pltpu.roll(wide[8 * q : 8 * q + 8], total * q, 1)
        packed = jnp.where((lane >= total * q) & (lane < total * (q + 1)), moved, packed)

    def sum_over(axis, value, buf, send, recv):
        mine = me[axis]
        buf[mine] = value

        def share(source, target):
            return pltpu.make_async_remote_copy(
                src_ref=buf.at[source], dst_ref=buf.at[source], send_sem=send.at[target],
                recv_sem=recv.at[source], device_id={axis: target}, device_id_type=MESH,
            )

        @pl.loop(1, counts[axis])
        def _(step):
            share(mine, peer(axis, step)).start()

        @pl.loop(1, counts[axis])
        def _(step):
            share(peer(axis, step), peer(axis, step)).wait_recv()

        result = buf[0]
        for index in range(1, counts[axis]):
            result = result + buf[index]
        return result

    packed = sum_over("gy", packed, sums_gy, gy_send, gy_recv)
    packed = sum_over("band", packed, sums_band, band_send, band_recv)
    packed = sum_over("gx", packed, sums_gx, gx_send, gx_recv)
    cells_all = float(n_x * n_y * n_z * n_gx * n_gy)
    packed = packed * (1.0 / cells_all)

    tiles = []
    for q in range(groups):
        tile = packed if q == 0 else pltpu.roll(packed, n_z - total * q, 1)
        eye = jnp.where(lax.rem(lane, total) == row + 8 * q, 1.0, 0.0)
        tiles.append(jnp.where(lane < total, tile, eye))
    for k in range(total):
        home, at = k // 8, k % 8
        pivot_row = tiles[home][at : at + 1, :]
        scaled = pivot_row * (1.0 / pivot_row[:, k : k + 1])
        for q in range(home, groups):
            column = tiles[q][:, k : k + 1]
            if q == home:
                column = jnp.where(row[:, :1] > at, column, 0.0)
            tiles[q] = tiles[q] - column * scaled
    for q in range(groups):
        diagonal = jnp.sum(jnp.where(lane == row + 8 * q, tiles[q], 0.0), axis=1, keepdims=True)
        tiles[q] = jnp.where(lane < total, 0.0, tiles[q] * lax.rsqrt(diagonal))
    inverse = jnp.concatenate(tiles, axis=0)
    lane_all = lax.broadcasted_iota(jnp.int32, (total, n_z), 1)
    high, middle, low = [part.astype(jnp.float32) for part in split_three(inverse)]
    left = jnp.concatenate(
        [
            jnp.where(lane_all < 3 * total, high, middle),
            jnp.where(lane_all < 2 * total, middle, jnp.where(lane_all < 3 * total, high, low)),
        ],
        axis=1,
    ).astype(jnp.bfloat16)
    for y in range(n_y):
        f_high, f_middle, f_low = parts[y]
        right = jnp.concatenate(
            [f_high, f_high, f_middle, f_high, f_high, f_middle, f_low, f_high], axis=0
        )
        rb[pl.ds(y, total, stride=n_y), :] = jnp.dot(
            left, right, preferred_element_type=jnp.float32
        )

    def collect(source, target):
        return pltpu.make_async_remote_copy(
            src_ref=rb.at[rows_of(target)], dst_ref=ob.at[source],
            send_sem=b_send.at[target], recv_sem=b_recv.at[source],
            device_id={"band": target}, device_id_type=MESH,
        )

    @pl.loop(1, n_band)
    def _(step):
        collect(band, peer("band", step)).start()

    ob[band] = rb[rows_of(band)]

    for r in range(3):
        @pl.loop(0, n_orb)
        def _(o, r=r):
            for copy in halo(r, o):
                copy.wait_send()

    @pl.loop(1, n_band)
    def _(step):
        spread(band, peer("band", step)).wait_send()

    for axis, buf, send, recv in (
        ("gy", sums_gy, gy_send, gy_recv),
        ("band", sums_band, band_send, band_recv),
        ("gx", sums_gx, gx_send, gx_recv),
    ):
        @pl.loop(1, counts[axis])
        def _(step, axis=axis, buf=buf, send=send, recv=recv):
            target = peer(axis, step)
            pltpu.make_async_remote_copy(
                src_ref=buf.at[me[axis]], dst_ref=buf.at[me[axis]], send_sem=send.at[target],
                recv_sem=recv.at[me[axis]], device_id={axis: target}, device_id_type=MESH,
            ).wait_send()

    @pl.loop(1, n_band)
    def _(step):
        collect(band, peer("band", step)).wait_send()
        collect(peer("band", step), peer("band", step)).wait_recv()

    for o in range(n_orb):
        out_ref[o] = ob[:, o * n_y : (o + 1) * n_y]


def local(orbitals, potential, sizes):
    n_gx, n_gy, n_band = sizes
    n_orb, n_x, n_y, n_z = orbitals.shape
    total = n_orb * n_band
    f32 = jnp.float32
    dma = pltpu.SemaphoreType.DMA
    vmem = pl.BlockSpec(memory_space=pltpu.VMEM)
    return pl.pallas_call(
        functools.partial(kernel, sizes),
        out_shape=jax.ShapeDtypeStruct(orbitals.shape, f32),
        in_specs=[pl.BlockSpec(memory_space=pl.ANY), vmem],
        out_specs=vmem,
        scratch_shapes=[
            pltpu.VMEM((3, n_orb, n_x + 2 * REACH, n_y, n_z), f32),
            pltpu.VMEM((3, n_orb, n_x, 3 * n_y, n_z), f32),
            pltpu.VMEM((n_orb, n_x, n_y, n_z), f32),
            pltpu.VMEM((n_x, n_orb * n_y, n_z), f32),
            pltpu.VMEM((total * n_y, n_z), f32),
            pltpu.VMEM((total * n_y, n_z), f32),
            pltpu.VMEM((n_x, n_orb * n_y, n_z), f32),
            pltpu.VMEM((n_gy, 8, n_z), f32),
            pltpu.VMEM((n_band, 8, n_z), f32),
            pltpu.VMEM((n_gx, 8, n_z), f32),
            pltpu.VMEM((total, n_z), f32),
            dma((2,)),
            dma((3, 2, n_orb)), dma((3, 2, n_orb)), dma((3, 2, n_orb)), dma((3, 2, n_orb)),
            dma((n_band,)), dma((n_band,)), dma((n_band,)), dma((n_band,)),
            dma((n_gy,)), dma((n_gy,)), dma((n_band,)), dma((n_band,)),
            dma((n_gx,)), dma((n_gx,)),
        ],
        compiler_params=pltpu.CompilerParams(
            collective_id=0, has_side_effects=True, vmem_limit_bytes=24 * 1024 * 1024
        ),
        cost_estimate=pl.CostEstimate(
            flops=16_000_000, bytes_accessed=4 * 2 * orbitals.size, transcendentals=0
        ),
    )(orbitals, potential)


def solution(mesh):
    sizes = tuple(mesh.shape[axis] for axis in ("gx", "gy", "band"))
    in_specs = (P("band", "gx", "gy", None), P("gx", "gy", None))
    out_specs = P("band", "gx", "gy", None)
    return jax.shard_map(
        functools.partial(local, sizes=sizes),
        mesh=mesh, in_specs=in_specs, out_specs=out_specs, check_vma=False,
    )
```

time: 630 us -> 70.4 us (0.11)
  blocking collectives: 494 us -> 0 us
  Pallas kernels: 0 us -> 67 us
  waiting for transfers between devices: 58.7 us -> 0 us
  starting transfers between devices: 44.9 us -> 0 us
  between operations: 13.6 us -> 0.01 us
  other arithmetic: 9.55 us -> 0 us
    psum x1 -> x0, blocking collectives: 494 us -> none  [local(): intersection = lax.psum(partial_sum, ('gx', 'gy')) / cells_all]
    pallas_call x0 -> x1, Pallas kernels: none -> 67 us  [local(): pl.pallas_call(functools.partial(kernel, sizes), out_shape=jax.ShapeDtype...]
    ppermute x12 -> x0, starting transfers between devices: 44.9 us -> none  [the longest x6 33.6 us: with_halo(): lax.ppermute(lax.slice_in_dim(block, 0, width, axis=dim), axis, backward)]
    all_gather x1 -> x0, waiting for transfers between devices: 36.6 us -> none  [local(): every = lax.all_gather(flat, 'band', axis=0, tiled=True)]
    ppermute x12 -> x0, waiting for transfers between devices: 22.1 us -> none  [the longest x6 13.4 us: with_halo(): lax.ppermute(lax.slice_in_dim(block, 0, width, axis=dim), axis, backward)]
    another operation x5 -> x0, other arithmetic: 6.68 us -> none  [the longest x3 3.59 us: local(): lower = jnp.linalg.cholesky(intersection)]
  transfers between devices with their start and end apart: 13 -> 0, of which waited for: 11 -> 0; matrix products, arithmetic and copies ran while one was open for 0% -> 0% of each run, Pallas kernels for 0% -> 0%
where the time goes in v1:
time: 70.4 us; the launch traced here: 69.3 us
  Pallas kernels  67 us (95%)
  local copies, waits for them, and re-layouts  2.32 us (3%)
    pallas_call x1, Pallas kernels, local(): pl.pallas_call(functools.partial(kernel, sizes), out_shape=jax.ShapeDtype...  67 us
    unnamed x5, local copies, waits for them, and re-layouts  2.32 us

profile of v1, /device:TPU:1, one launch (start us, length us, event | category | flops | bytes accessed | tf_op | source)
XLA Modules:
  0.0 69.3 jit_solution(2299207519046232084)
XLA Ops:
  0.0 0.0 copy-start
  0.0 0.9 %copy-done = f32[4,8,8,128]{3,2,1,0:T(8,128)S(1)} copy-done((f32[4,8,8,128]{3,2,1,0:T(8,128)S(1)}, f32[4,8,8,128]{3,2,1,0:T(8,128)}, u32[]{:S(2)}) %copy-start) | copy-done | bytes 131096
  0.9 0.0 copy-start.1
  0.9 0.8 %copy-done.1 = f32[8,8,128]{2,1,0:T(8,128)S(1)} copy-done((f32[8,8,128]{2,1,0:T(8,128)S(1)}, f32[8,8,128]{2,1,0:T(8,128)}, u32[]{:S(2)}) %copy-start.1) | copy-done | bytes 32792
  1.7 67.0 %shard_map.28 = f32[4,8,8,128]{3,2,1,0:T(8,128)S(1)} custom-call(f32[4,8,8,128]{3,2,1,0:T(8,128)S(1)} %copy-done, f32[8,8,128]{2,1,0:T(8,128)S(1)} %copy-done.1), custom_call_target="tpu_custom_call" | custom-call | flops 16000000 | bytes 262144 | tf_op jit(solution)/shard_map/pallas_call | solution.py:316
  68.6 0.7 copy.4
Async XLA Ops:
  0.0 0.9 %copy-start = (f32[4,8,8,128]{3,2,1,0:T(8,128)S(1)}, f32[4,8,8,128]{3,2,1,0:T(8,128)}, u32[]{:S(2)}) copy-start(f32[4,8,8,128]{3,2,1,0:T(8,128)} %orb_ref.1) | copy-start | bytes 393220
  0.9 0.8 %copy-start.1 = (f32[8,8,128]{2,1,0:T(8,128)S(1)}, f32[8,8,128]{2,1,0:T(8,128)}, u32[]{:S(2)}) copy-start(f32[8,8,128]{2,1,0:T(8,128)} %pot_ref.1) | copy-start | bytes 98308

commit v2 on v1

--- a/solution.py
+++ b/solution.py
@@ -48,9 +48,10 @@
 
 
 def kernel(
-    sizes, orb_ref, pot_ref, out_ref, xb, yb, acc, fown, fc, rb, ob, sums_gy, sums_band, sums_gx, gram,
+    sizes, orb_ref, pot_hbm, out_ref, pot_ref, xb, yb, acc, fown, fc, rb, ob, sums_gy, sums_band, sums_gx, gram,
     load_sem, x_send, x_recv, y_send, y_recv, a_send, a_recv, b_send, b_recv,
     gy_send, gy_recv, band_send, band_recv, gx_send, gx_recv,
+    near, middle_way, far,
 ):
     n_gx, n_gy, n_band = sizes
     n_orb, n_x, n_y, n_z = out_ref.shape
@@ -65,22 +66,27 @@
         return lax.rem(me[axis] + step, counts[axis])
 
     barrier = pltpu.get_barrier_semaphore()
+
+    def greet(semaphore, axis, distance):
+        for step in (distance, counts[axis] - distance):
+            pl.semaphore_signal(
+                semaphore, inc=1, device_id={axis: peer(axis, step)}, device_id_type=MESH
+            )
+
     for axis in ("gx", "gy", "band"):
-        @pl.loop(1, counts[axis])
-        def _(step, axis=axis):
-            pl.semaphore_signal(
-                barrier, inc=1, device_id={axis: peer(axis, step)}, device_id_type=MESH
-            )
+        greet(barrier, axis, 1)
 
     own_x = pl.ds(REACH, n_x)
     own_y = pl.ds(n_y, n_y)
     load_x = pltpu.make_async_copy(orb_ref, xb.at[0, :, own_x], load_sem.at[0])
     load_y = pltpu.make_async_copy(orb_ref, yb.at[0, :, :, own_y], load_sem.at[1])
+    load_pot = pltpu.make_async_copy(pot_hbm, pot_ref, load_sem.at[2])
     load_x.start()
     load_y.start()
+    load_pot.start()
     load_x.wait()
     load_y.wait()
-    pl.semaphore_wait(barrier, n_gx + n_gy + n_band - 3)
+    pl.semaphore_wait(barrier, 6)
 
     def halo(r, o):
         right_x = {"gx": peer("gx", 1)}
@@ -135,11 +141,44 @@
         for copy in halo(0, o):
             copy.start()
 
+    greet(near, "band", 1)
+    load_pot.wait()
+
     @pl.loop(0, n_orb)
     def _(o):
         local_part(0, o)
 
+    depth = n_orb * n_y
+
+    def rows_of(index):
+        return pl.ds(pl.multiple_of(depth * index, depth), depth)
+
+    def spread(target, o):
+        start = pl.multiple_of(o * n_y, n_y)
+        return pltpu.make_async_remote_copy(
+            src_ref=fown.at[target, pl.ds(start, n_y)],
+            dst_ref=fc.at[pl.ds(pl.multiple_of(depth * band + start, n_y), n_y)],
+            send_sem=a_send.at[target], recv_sem=a_recv.at[band],
+            device_id={"band": target}, device_id_type=MESH,
+        )
+
+    def spread_whole(source, target):
+        return pltpu.make_async_remote_copy(
+            src_ref=fown.at[target], dst_ref=fc.at[rows_of(source)],
+            send_sem=a_send.at[target], recv_sem=a_recv.at[source],
+            device_id={"band": target}, device_id_type=MESH,
+        )
+
+    def by_distance(count):
+        return sorted(range(1, count), key=lambda step: min(step, count - step))
+
     for r in range(3):
+        if r == 1:
+            pl.semaphore_wait(near, 2)
+            greet(middle_way, "band", 2)
+        if r == 2:
+            pl.semaphore_wait(middle_way, 2)
+
         @pl.loop(0, n_orb)
         def _(o, r=r):
             for copy in halo(r, o):
@@ -153,28 +192,14 @@
                 local_part(r + 1, o)
             else:
                 fown[:, pl.ds(pl.multiple_of(o * n_y, n_y), n_y)] = result
-
-    depth = n_orb * n_y
-
-    def rows_of(index):
-        return pl.ds(pl.multiple_of(depth * index, depth), depth)
-
-    def spread(source, target):
-        return pltpu.make_async_remote_copy(
-            src_ref=fown.at[target], dst_ref=fc.at[rows_of(source)],
-            send_sem=a_send.at[target], recv_sem=a_recv.at[source],
-            device_id={"band": target}, device_id_type=MESH,
-        )
-
-    @pl.loop(1, n_band)
-    def _(step):
-        spread(band, peer("band", step)).start()
-
+                for step in reversed(by_distance(n_band)):
+                    spread(peer("band", step), o).start()
+
+    if n_gx > 8:
+        greet(far, "gx", 4)
     fc[rows_of(band)] = fown[band]
-
-    @pl.loop(1, n_band)
-    def _(step):
-        spread(peer("band", step), peer("band", step)).wait_recv()
+    for step in by_distance(n_band):
+        spread_whole(peer("band", step), band).wait_recv()
 
     parts = []
     for y in range(n_y):
@@ -197,30 +222,25 @@
         packed = jnp.where((lane >= total * q) & (lane < total * (q + 1)), moved, packed)
 
     def sum_over(axis, value, buf, send, recv):
-        mine = me[axis]
-        buf[mine] = value
-
-        def share(source, target):
+        buf[0] = value
+
+        def share(step):
             return pltpu.make_async_remote_copy(
-                src_ref=buf.at[source], dst_ref=buf.at[source], send_sem=send.at[target],
-                recv_sem=recv.at[source], device_id={axis: target}, device_id_type=MESH,
+                src_ref=buf.at[0], dst_ref=buf.at[step], send_sem=send.at[step],
+                recv_sem=recv.at[step], device_id={axis: peer(axis, step)}, device_id_type=MESH,
             )
 
-        @pl.loop(1, counts[axis])
-        def _(step):
-            share(mine, peer(axis, step)).start()
-
-        @pl.loop(1, counts[axis])
-        def _(step):
-            share(peer(axis, step), peer(axis, step)).wait_recv()
-
-        result = buf[0]
-        for index in range(1, counts[axis]):
-            result = result + buf[index]
-        return result
+        for step in reversed(by_distance(counts[axis])):
+            share(step).start()
+        for step in by_distance(counts[axis]):
+            share(step).wait_recv()
+            value = value + buf[step]
+        return value
 
     packed = sum_over("gy", packed, sums_gy, gy_send, gy_recv)
     packed = sum_over("band", packed, sums_band, band_send, band_recv)
+    if n_gx > 8:
+        pl.semaphore_wait(far, 2)
     packed = sum_over("gx", packed, sums_gx, gx_send, gx_recv)
     cells_all = float(n_x * n_y * n_z * n_gx * n_gy)
     packed = packed * (1.0 / cells_all)
@@ -268,8 +288,7 @@
             device_id={"band": target}, device_id_type=MESH,
         )
 
-    @pl.loop(1, n_band)
-    def _(step):
+    for step in reversed(by_distance(n_band)):
         collect(band, peer("band", step)).start()
 
     ob[band] = rb[rows_of(band)]
@@ -282,7 +301,7 @@
 
     @pl.loop(1, n_band)
     def _(step):
-        spread(band, peer("band", step)).wait_send()
+        spread_whole(band, peer("band", step)).wait_send()
 
     for axis, buf, send, recv in (
         ("gy", sums_gy, gy_send, gy_recv),
@@ -291,10 +310,9 @@
     ):
         @pl.loop(1, counts[axis])
         def _(step, axis=axis, buf=buf, send=send, recv=recv):
-            target = peer(axis, step)
             pltpu.make_async_remote_copy(
-                src_ref=buf.at[me[axis]], dst_ref=buf.at[me[axis]], send_sem=send.at[target],
-                recv_sem=recv.at[me[axis]], device_id={axis: target}, device_id_type=MESH,
+                src_ref=buf.at[0], dst_ref=buf.at[step], send_sem=send.at[step],
+                recv_sem=recv.at[step], device_id={axis: peer(axis, step)}, device_id_type=MESH,
             ).wait_send()
 
     @pl.loop(1, n_band)
@@ -316,9 +334,10 @@
     return pl.pallas_call(
         functools.partial(kernel, sizes),
         out_shape=jax.ShapeDtypeStruct(orbitals.shape, f32),
-        in_specs=[pl.BlockSpec(memory_space=pl.ANY), vmem],
+        in_specs=[pl.BlockSpec(memory_space=pl.ANY)] * 2,
         out_specs=vmem,
         scratch_shapes=[
+            pltpu.VMEM((n_x, n_y, n_z), f32),
             pltpu.VMEM((3, n_orb, n_x + 2 * REACH, n_y, n_z), f32),
             pltpu.VMEM((3, n_orb, n_x, 3 * n_y, n_z), f32),
             pltpu.VMEM((n_orb, n_x, n_y, n_z), f32),
@@ -330,14 +349,15 @@
             pltpu.VMEM((n_band, 8, n_z), f32),
             pltpu.VMEM((n_gx, 8, n_z), f32),
             pltpu.VMEM((total, n_z), f32),
-            dma((2,)),
+            dma((3,)),
             dma((3, 2, n_orb)), dma((3, 2, n_orb)), dma((3, 2, n_orb)), dma((3, 2, n_orb)),
             dma((n_band,)), dma((n_band,)), dma((n_band,)), dma((n_band,)),
             dma((n_gy,)), dma((n_gy,)), dma((n_band,)), dma((n_band,)),
             dma((n_gx,)), dma((n_gx,)),
+            *[pltpu.SemaphoreType.REGULAR] * 3,
         ],
         compiler_params=pltpu.CompilerParams(
-            collective_id=0, has_side_effects=True, vmem_limit_bytes=24 * 1024 * 1024
+            collective_id=0, has_side_effects=True, vmem_limit_bytes=56 * 1024 * 1024
         ),
         cost_estimate=pl.CostEstimate(
             flops=16_000_000, bytes_accessed=4 * 2 * orbitals.size, transcendentals=0

time: 70.4 us -> 61.7 us (0.88)
  Pallas kernels: 67 us -> 59.4 us
  local copies, waits for them, and re-layouts: 2.32 us -> 1.57 us
    pallas_call x1, Pallas kernels: 67 us -> 59.4 us  [local(): pl.pallas_call(functools.partial(kernel, sizes), out_shape=jax.ShapeDtype...]
    unnamed x5 -> x1, local copies, waits for them, and re-layouts: 2.32 us -> 1.57 us
where the time goes in v2:
time: 61.7 us; the launch traced here: 61 us
  Pallas kernels  59.4 us (96%)
  local copies, waits for them, and re-layouts  1.57 us (3%)
    pallas_call x1, Pallas kernels, local(): pl.pallas_call(functools.partial(kernel, sizes), out_shape=jax.ShapeDtype...  59.4 us
    unnamed x1, local copies, waits for them, and re-layouts  1.57 us

profile of v2, /device:TPU:1, one launch (start us, length us, event | category | flops | bytes accessed | tf_op | source)
XLA Modules:
  0.0 61.0 jit_solution(3649438730474220802)
XLA Ops:
  0.0 59.4 %shard_map.28 = f32[4,8,8,128]{3,2,1,0:T(8,128)} custom-call(f32[4,8,8,128]{3,2,1,0:T(8,128)} %orb_ref.1, f32[8,8,128]{2,1,0:T(8,128)} %pot_hbm.1), custom_call_target="tpu_custom_call" | custom-call | flops 16000000 | bytes 262144 | tf_op jit(solution)/shard_map/pallas_call | solution.py:334
  59.4 1.6 %copy.4 = f32[4,8,8,128]{3,2,1,0:T(8,128)} copy(f32[4,8,8,128]{3,2,1,0:T(8,128)} %shard_map.28) | data formatting | bytes 262144

commit v3 on v2

--- a/solution.py
+++ b/solution.py
@@ -169,8 +169,36 @@
             device_id={"band": target}, device_id_type=MESH,
         )
 
+    def share(step, where, buf, send, recv):
+        return pltpu.make_async_remote_copy(
+            src_ref=buf.at[0], dst_ref=buf.at[step], send_sem=send.at[step],
+            recv_sem=recv.at[step], device_id=where(step), device_id_type=MESH,
+        )
+
     def by_distance(count):
         return sorted(range(1, count), key=lambda step: min(step, count - step))
+
+    other_core = gy + 1 - 2 * lax.rem(gy, 2)
+    band_steps = [0] + by_distance(n_band)
+    phases = (
+        (
+            [2 * step + core for step in band_steps for core in (0, 1) if step + core > 0],
+            lambda step: {
+                "gy": other_core if step % 2 else gy, "band": peer("band", step // 2)
+            },
+            sums_band, band_send, band_recv,
+        ),
+        (
+            by_distance(n_gy // 2),
+            lambda step: {"gy": peer("gy", 2 * step)},
+            sums_gy, gy_send, gy_recv,
+        ),
+        (
+            by_distance(n_gx),
+            lambda step: {"gx": peer("gx", step)},
+            sums_gx, gx_send, gx_recv,
+        ),
+    )
 
     for r in range(3):
         if r == 1:
@@ -221,27 +249,20 @@
         moved = pltpu.roll(wide[8 * q : 8 * q + 8], total * q, 1)
         packed = jnp.where((lane >= total * q) & (lane < total * (q + 1)), moved, packed)
 
-    def sum_over(axis, value, buf, send, recv):
+    def sum_over(steps, where, value, buf, send, recv):
         buf[0] = value
-
-        def share(step):
-            return pltpu.make_async_remote_copy(
-                src_ref=buf.at[0], dst_ref=buf.at[step], send_sem=send.at[step],
-                recv_sem=recv.at[step], device_id={axis: peer(axis, step)}, device_id_type=MESH,
-            )
-
-        for step in reversed(by_distance(counts[axis])):
-            share(step).start()
-        for step in by_distance(counts[axis]):
-            share(step).wait_recv()
+        for step in reversed(steps):
+            share(step, where, buf, send, recv).start()
+        for step in steps:
+            share(step, where, buf, send, recv).wait_recv()
             value = value + buf[step]
         return value
 
-    packed = sum_over("gy", packed, sums_gy, gy_send, gy_recv)
-    packed = sum_over("band", packed, sums_band, band_send, band_recv)
+    packed = sum_over(*phases[0][:2], packed, *phases[0][2:])
+    packed = sum_over(*phases[1][:2], packed, *phases[1][2:])
     if n_gx > 8:
         pl.semaphore_wait(far, 2)
-    packed = sum_over("gx", packed, sums_gx, gx_send, gx_recv)
+    packed = sum_over(*phases[2][:2], packed, *phases[2][2:])
     cells_all = float(n_x * n_y * n_z * n_gx * n_gy)
     packed = packed * (1.0 / cells_all)
 
@@ -250,15 +271,26 @@
         tile = packed if q == 0 else pltpu.roll(packed, n_z - total * q, 1)
         eye = jnp.where(lax.rem(lane, total) == row + 8 * q, 1.0, 0.0)
         tiles.append(jnp.where(lane < total, tile, eye))
-    for k in range(total):
-        home, at = k // 8, k % 8
-        pivot_row = tiles[home][at : at + 1, :]
-        scaled = pivot_row * (1.0 / pivot_row[:, k : k + 1])
-        for q in range(home, groups):
-            column = tiles[q][:, k : k + 1]
-            if q == home:
-                column = jnp.where(row[:, :1] > at, column, 0.0)
-            tiles[q] = tiles[q] - column * scaled
+    for home in range(groups):
+        columns = [
+            [
+                jnp.broadcast_to(tiles[q][:, 8 * home + at : 8 * home + at + 1], (8, n_z))
+                for q in range(home, groups)
+            ]
+            for at in range(8)
+        ]
+        for at in range(8):
+            pivot_row = jnp.broadcast_to(tiles[home][at : at + 1, :], (8, n_z))
+            reciprocal = 1.0 / jnp.broadcast_to(columns[at][0][at : at + 1, :], (8, n_z))
+            factors = [column * reciprocal for column in columns[at]]
+            factors[0] = jnp.where(row > at, factors[0], 0.0)
+            for factor, q in zip(factors, range(home, groups)):
+                tiles[q] = tiles[q] - factor * pivot_row
+            for later in range(at + 1, 8):
+                value = jnp.broadcast_to(columns[later][0][at : at + 1, :], (8, n_z))
+                columns[later] = [
+                    column - factor * value for column, factor in zip(columns[later], factors)
+                ]
     for q in range(groups):
         diagonal = jnp.sum(jnp.where(lane == row + 8 * q, tiles[q], 0.0), axis=1, keepdims=True)
         tiles[q] = jnp.where(lane < total, 0.0, tiles[q] * lax.rsqrt(diagonal))
@@ -303,17 +335,9 @@
     def _(step):
         spread_whole(band, peer("band", step)).wait_send()
 
-    for axis, buf, send, recv in (
-        ("gy", sums_gy, gy_send, gy_recv),
-        ("band", sums_band, band_send, band_recv),
-        ("gx", sums_gx, gx_send, gx_recv),
-    ):
-        @pl.loop(1, counts[axis])
-        def _(step, axis=axis, buf=buf, send=send, recv=recv):
-            pltpu.make_async_remote_copy(
-                src_ref=buf.at[0], dst_ref=buf.at[step], send_sem=send.at[step],
-                recv_sem=recv.at[step], device_id={axis: peer(axis, step)}, device_id_type=MESH,
-            ).wait_send()
+    for steps, where, buf, send, recv in phases:
+        for step in steps:
+            share(step, where, buf, send, recv).wait_send()
 
     @pl.loop(1, n_band)
     def _(step):
@@ -345,19 +369,19 @@
             pltpu.VMEM((total * n_y, n_z), f32),
             pltpu.VMEM((total * n_y, n_z), f32),
             pltpu.VMEM((n_x, n_orb * n_y, n_z), f32),
-            pltpu.VMEM((n_gy, 8, n_z), f32),
-            pltpu.VMEM((n_band, 8, n_z), f32),
+            pltpu.VMEM((n_gy // 2, 8, n_z), f32),
+            pltpu.VMEM((2 * n_band, 8, n_z), f32),
             pltpu.VMEM((n_gx, 8, n_z), f32),
             pltpu.VMEM((total, n_z), f32),
             dma((3,)),
             dma((3, 2, n_orb)), dma((3, 2, n_orb)), dma((3, 2, n_orb)), dma((3, 2, n_orb)),
             dma((n_band,)), dma((n_band,)), dma((n_band,)), dma((n_band,)),
-            dma((n_gy,)), dma((n_gy,)), dma((n_band,)), dma((n_band,)),
+            dma((n_gy // 2,)), dma((n_gy // 2,)), dma((2 * n_band,)), dma((2 * n_band,)),
             dma((n_gx,)), dma((n_gx,)),
             *[pltpu.SemaphoreType.REGULAR] * 3,
         ],
         compiler_params=pltpu.CompilerParams(
-            collective_id=0, has_side_effects=True, vmem_limit_bytes=56 * 1024 * 1024
+            collective_id=0, has_side_effects=True, vmem_limit_bytes=55008 * 1024
         ),
         cost_estimate=pl.CostEstimate(
             flops=16_000_000, bytes_accessed=4 * 2 * orbitals.size, transcendentals=0

time: 61.7 us -> 59.4 us (0.963)
  the two profiles are of different devices: /device:TPU:1 before, /device:TPU:8 now
where the time goes in v3:
time: 59.4 us; the launch traced here: 59.2 us
  Pallas kernels  57.7 us (97%)
  local copies, waits for them, and re-layouts  1.42 us (2%)
    pallas_call x1, Pallas kernels, local(): pl.pallas_call(functools.partial(kernel, sizes), out_shape=jax.ShapeDtype...  57.7 us
    unnamed x3, local copies, waits for them, and re-layouts  1.42 us

profile of v3, /device:TPU:8, one launch (start us, length us, event | category | flops | bytes accessed | tf_op | source)
XLA Modules:
  0.0 59.2 jit_solution(13005630400489499351)
XLA Ops:
  0.0 0.0 copy-start
  0.0 0.8 %copy-done = f32[8,8,128]{2,1,0:T(8,128)S(1)} copy-done((f32[8,8,128]{2,1,0:T(8,128)S(1)}, f32[8,8,128]{2,1,0:T(8,128)}, u32[]{:S(2)}) %copy-start) | copy-done | bytes 32792
  0.8 57.7 %shard_map.28 = f32[4,8,8,128]{3,2,1,0:T(8,128)S(1)} custom-call(f32[4,8,8,128]{3,2,1,0:T(8,128)} %orb_ref.1, f32[8,8,128]{2,1,0:T(8,128)S(1)} %copy-done), custom_call_target="tpu_custom_call" | custom-call | flops 16000000 | bytes 262144 | tf_op jit(solution)/shard_map/pallas_call | solution.py:358
  58.5 0.7 %copy.4 = f32[4,8,8,128]{3,2,1,0:T(8,128)} copy(f32[4,8,8,128]{3,2,1,0:T(8,128)S(1)} %shard_map.28) | data formatting | bytes 262144
Async XLA Ops:
  0.0 0.8 %copy-start = (f32[8,8,128]{2,1,0:T(8,128)S(1)}, f32[8,8,128]{2,1,0:T(8,128)}, u32[]{:S(2)}) copy-start(f32[8,8,128]{2,1,0:T(8,128)} %pot_hbm.1) | copy-start | bytes 98308

commit v4 on v3

--- a/solution.py
+++ b/solution.py
@@ -48,8 +48,8 @@
 
 
 def kernel(
-    sizes, orb_ref, pot_hbm, out_ref, pot_ref, xb, yb, acc, fown, fc, rb, ob, sums_gy, sums_band, sums_gx, gram,
-    load_sem, x_send, x_recv, y_send, y_recv, a_send, a_recv, b_send, b_recv,
+    sizes, orb_ref, pot_hbm, out_ref, pot_ref, xb, yb, acc, every, fc, sums_gy, sums_band, sums_gx, gram,
+    load_sem, x_send, x_recv, y_send, y_recv, a_send, a_recv, ring_send, ring_recv,
     gy_send, gy_recv, band_send, band_recv, gx_send, gx_recv,
     near, middle_way, far,
 ):
@@ -103,14 +103,14 @@
         every = slice(None)
         return (
             move(xb, (r, o, pl.ds(n_x, REACH)), (r, o, pl.ds(0, REACH)),
-                 x_send.at[r, 0, o], x_recv.at[r, 0, o], right_x),
+                 x_send.at[r, 0], x_recv.at[r, 0, o], right_x),
             move(xb, (r, o, pl.ds(REACH, REACH)), (r, o, pl.ds(n_x + REACH, REACH)),
-                 x_send.at[r, 1, o], x_recv.at[r, 1, o], left_x),
+                 x_send.at[r, 1], x_recv.at[r, 1, o], left_x),
             move(yb, (r, o, every, pl.ds(2 * n_y - REACH, REACH)),
                  (r, o, every, pl.ds(n_y - REACH, REACH)),
-                 y_send.at[r, 0, o], y_recv.at[r, 0, o], right_y),
+                 y_send.at[r, 0], y_recv.at[r, 0, o], right_y),
             move(yb, (r, o, every, pl.ds(n_y, REACH)), (r, o, every, pl.ds(2 * n_y, REACH)),
-                 y_send.at[r, 1, o], y_recv.at[r, 1, o], left_y),
+                 y_send.at[r, 1], y_recv.at[r, 1, o], left_y),
         )
 
     def local_part(r, o):
@@ -156,7 +156,7 @@
     def spread(target, o):
         start = pl.multiple_of(o * n_y, n_y)
         return pltpu.make_async_remote_copy(
-            src_ref=fown.at[target, pl.ds(start, n_y)],
+            src_ref=every.at[band, target, pl.ds(start, n_y)],
             dst_ref=fc.at[pl.ds(pl.multiple_of(depth * band + start, n_y), n_y)],
             send_sem=a_send.at[target], recv_sem=a_recv.at[band],
             device_id={"band": target}, device_id_type=MESH,
@@ -164,7 +164,7 @@
 
     def spread_whole(source, target):
         return pltpu.make_async_remote_copy(
-            src_ref=fown.at[target], dst_ref=fc.at[rows_of(source)],
+            src_ref=every.at[band, target], dst_ref=fc.at[rows_of(source)],
             send_sem=a_send.at[target], recv_sem=a_recv.at[source],
             device_id={"band": target}, device_id_type=MESH,
         )
@@ -219,13 +219,13 @@
                     copy.start()
                 local_part(r + 1, o)
             else:
-                fown[:, pl.ds(pl.multiple_of(o * n_y, n_y), n_y)] = result
+                every[band, :, pl.ds(pl.multiple_of(o * n_y, n_y), n_y)] = result
                 for step in reversed(by_distance(n_band)):
                     spread(peer("band", step), o).start()
 
     if n_gx > 8:
         greet(far, "gx", 4)
-    fc[rows_of(band)] = fown[band]
+    fc[rows_of(band)] = every[band, band]
     for step in by_distance(n_band):
         spread_whole(peer("band", step), band).wait_recv()
 
@@ -249,20 +249,66 @@
         moved = pltpu.roll(wide[8 * q : 8 * q + 8], total * q, 1)
         packed = jnp.where((lane >= total * q) & (lane < total * (q + 1)), moved, packed)
 
-    def sum_over(steps, where, value, buf, send, recv):
+    def sum_sends(steps, where, value, buf, send, recv):
         buf[0] = value
         for step in reversed(steps):
             share(step, where, buf, send, recv).start()
+
+    def sum_waits(steps, where, value, buf, send, recv):
         for step in steps:
             share(step, where, buf, send, recv).wait_recv()
             value = value + buf[step]
         return value
 
-    packed = sum_over(*phases[0][:2], packed, *phases[0][2:])
-    packed = sum_over(*phases[1][:2], packed, *phases[1][2:])
+    half = n_band // 2
+
+    def ring(direction, distance, source):
+        width = n_x // 2 if distance == half else n_x
+        block = every.at[source, pl.ds(direction * (n_x - width), width)]
+        return pltpu.make_async_remote_copy(
+            src_ref=block, dst_ref=block, send_sem=ring_send.at[direction, distance - 1],
+            recv_sem=ring_recv.at[direction, distance - 1],
+            device_id={"band": peer("band", n_band - 1 if direction else 1)},
+            device_id_type=MESH,
+        )
+
+    def source_at(direction, distance):
+        return peer("band", distance if direction else n_band - distance)
+
+    def pass_on(distance):
+        for direction in (0, 1):
+            source = source_at(direction, distance - 1)
+            if distance > 1:
+                ring(direction, distance - 1, source).wait_recv()
+            ring(direction, distance, source).start()
+
+    first, second, third = phases
+    sum_sends(*first[:2], packed, *first[2:])
+    pass_on(1)
+    packed = sum_waits(*first[:2], packed, *first[2:])
+    sum_sends(*second[:2], packed, *second[2:])
+    pass_on(2)
+    packed = sum_waits(*second[:2], packed, *second[2:])
     if n_gx > 8:
         pl.semaphore_wait(far, 2)
-    packed = sum_over(*phases[2][:2], packed, *phases[2][2:])
+    sum_sends(*third[:2], packed, *third[2:])
+    for r in range(3):
+        for buf, send in ((xb.at[r, :, pl.ds(0, REACH)], x_send),
+                          (yb.at[r, :, :, pl.ds(0, REACH)], y_send)):
+            for direction in (0, 1):
+                pltpu.make_async_remote_copy(
+                    src_ref=buf, dst_ref=buf, send_sem=send.at[r, direction],
+                    recv_sem=x_recv.at[0, 0, 0], device_id={"gx": peer("gx", 1)},
+                    device_id_type=MESH,
+                ).wait_send()
+    for step in by_distance(n_band):
+        spread_whole(band, peer("band", step)).wait_send()
+    for steps, where, buf, send, recv in phases[:2]:
+        for step in steps:
+            share(step, where, buf, send, recv).wait_send()
+    for distance in range(3, half + 1):
+        pass_on(distance)
+    packed = sum_waits(*third[:2], packed, *third[2:])
     cells_all = float(n_x * n_y * n_z * n_gx * n_gy)
     packed = packed * (1.0 / cells_all)
 
@@ -294,58 +340,30 @@
     for q in range(groups):
         diagonal = jnp.sum(jnp.where(lane == row + 8 * q, tiles[q], 0.0), axis=1, keepdims=True)
         tiles[q] = jnp.where(lane < total, 0.0, tiles[q] * lax.rsqrt(diagonal))
-    inverse = jnp.concatenate(tiles, axis=0)
-    lane_all = lax.broadcasted_iota(jnp.int32, (total, n_z), 1)
-    high, middle, low = [part.astype(jnp.float32) for part in split_three(inverse)]
-    left = jnp.concatenate(
-        [
-            jnp.where(lane_all < 3 * total, high, middle),
-            jnp.where(lane_all < 2 * total, middle, jnp.where(lane_all < 3 * total, high, low)),
-        ],
-        axis=1,
-    ).astype(jnp.bfloat16)
-    for y in range(n_y):
-        f_high, f_middle, f_low = parts[y]
-        right = jnp.concatenate(
-            [f_high, f_high, f_middle, f_high, f_high, f_middle, f_low, f_high], axis=0
-        )
-        rb[pl.ds(y, total, stride=n_y), :] = jnp.dot(
-            left, right, preferred_element_type=jnp.float32
-        )
-
-    def collect(source, target):
-        return pltpu.make_async_remote_copy(
-            src_ref=rb.at[rows_of(target)], dst_ref=ob.at[source],
-            send_sem=b_send.at[target], recv_sem=b_recv.at[source],
-            device_id={"band": target}, device_id_type=MESH,
-        )
-
-    for step in reversed(by_distance(n_band)):
-        collect(band, peer("band", step)).start()
-
-    ob[band] = rb[rows_of(band)]
-
-    for r in range(3):
-        @pl.loop(0, n_orb)
-        def _(o, r=r):
-            for copy in halo(r, o):
-                copy.wait_send()
-
-    @pl.loop(1, n_band)
-    def _(step):
-        spread_whole(band, peer("band", step)).wait_send()
-
-    for steps, where, buf, send, recv in phases:
-        for step in steps:
-            share(step, where, buf, send, recv).wait_send()
-
-    @pl.loop(1, n_band)
-    def _(step):
-        collect(band, peer("band", step)).wait_send()
-        collect(peer("band", step), peer("band", step)).wait_recv()
-
-    for o in range(n_orb):
-        out_ref[o] = ob[:, o * n_y : (o + 1) * n_y]
+    for q in range(groups):
+        gram[pl.ds(8 * q, 8), :] = tiles[q]
+    mine = gram[pl.ds(pl.multiple_of(8 * (band // 2), 8), 8), :]
+    mine = jnp.where(lax.rem(band, 2) == 1, pltpu.roll(mine, 4, 0), mine)
+    for direction in (0, 1):
+        ring(direction, half, source_at(direction, half)).wait_recv()
+    results = [[None] * n_x for _ in range(n_orb)]
+    for j in range(total):
+        source, o = j // n_orb, j % n_orb
+        column = jnp.broadcast_to(mine[:, total + j : total + j + 1], (8, n_z))
+        weights = [jnp.broadcast_to(column[i : i + 1, :], (8, n_z)) for i in range(n_orb)]
+        for x in range(n_x):
+            value = every[source, x, o * n_y : (o + 1) * n_y]
+            for i in range(n_orb):
+                term = weights[i] * value
+                results[i][x] = term if j == 0 else results[i][x] + term
+    for i in range(n_orb):
+        for x in range(n_x):
+            out_ref[i, x] = results[i][x]
+    for step in third[0]:
+        share(step, *third[1:]).wait_send()
+    for direction in (0, 1):
+        for distance in range(1, half + 1):
+            ring(direction, distance, source_at(direction, distance - 1)).wait_send()
 
 
 def local(orbitals, potential, sizes):
@@ -365,17 +383,15 @@
             pltpu.VMEM((3, n_orb, n_x + 2 * REACH, n_y, n_z), f32),
             pltpu.VMEM((3, n_orb, n_x, 3 * n_y, n_z), f32),
             pltpu.VMEM((n_orb, n_x, n_y, n_z), f32),
-            pltpu.VMEM((n_x, n_orb * n_y, n_z), f32),
+            pltpu.VMEM((n_band, n_x, n_orb * n_y, n_z), f32),
             pltpu.VMEM((total * n_y, n_z), f32),
-            pltpu.VMEM((total * n_y, n_z), f32),
-            pltpu.VMEM((n_x, n_orb * n_y, n_z), f32),
             pltpu.VMEM((n_gy // 2, 8, n_z), f32),
             pltpu.VMEM((2 * n_band, 8, n_z), f32),
             pltpu.VMEM((n_gx, 8, n_z), f32),
             pltpu.VMEM((total, n_z), f32),
             dma((3,)),
-            dma((3, 2, n_orb)), dma((3, 2, n_orb)), dma((3, 2, n_orb)), dma((3, 2, n_orb)),
-            dma((n_band,)), dma((n_band,)), dma((n_band,)), dma((n_band,)),
+            dma((3, 2)), dma((3, 2, n_orb)), dma((3, 2)), dma((3, 2, n_orb)),
+            dma((n_band,)), dma((n_band,)), dma((2, n_band // 2)), dma((2, n_band // 2)),
             dma((n_gy // 2,)), dma((n_gy // 2,)), dma((2 * n_band,)), dma((2 * n_band,)),
             dma((n_gx,)), dma((n_gx,)),
             *[pltpu.SemaphoreType.REGULAR] * 3,

time: 59.4 us -> 57.3 us (0.965)
  the two profiles are of different devices: /device:TPU:8 before, /device:TPU:2 now
where the time goes in v4:
time: 57.3 us; the launch traced here: 57.1 us
  Pallas kernels  55.6 us (97%)
  local copies, waits for them, and re-layouts  1.42 us (2%)
    pallas_call x1, Pallas kernels, local(): pl.pallas_call(functools.partial(kernel, sizes), out_shape=jax.ShapeDtype...  55.6 us
    unnamed x3, local copies, waits for them, and re-layouts  1.42 us

profile of v4, /device:TPU:2, one launch (start us, length us, event | category | flops | bytes accessed | tf_op | source)
XLA Modules:
  0.0 57.1 jit_solution(18085184851717632672)
XLA Ops:
  0.0 0.0 copy-start
  0.0 0.8 %copy-done = f32[8,8,128]{2,1,0:T(8,128)S(1)} copy-done((f32[8,8,128]{2,1,0:T(8,128)S(1)}, f32[8,8,128]{2,1,0:T(8,128)}, u32[]{:S(2)}) %copy-start) | copy-done | bytes 32792
  0.8 55.6 %shard_map.28 = f32[4,8,8,128]{3,2,1,0:T(8,128)S(1)} custom-call(f32[4,8,8,128]{3,2,1,0:T(8,128)} %orb_ref.1, f32[8,8,128]{2,1,0:T(8,128)S(1)} %copy-done), custom_call_target="tpu_custom_call" | custom-call | flops 16000000 | bytes 262144 | tf_op jit(solution)/shard_map/pallas_call | solution.py:376
  56.4 0.7 %copy.4 = f32[4,8,8,128]{3,2,1,0:T(8,128)} copy(f32[4,8,8,128]{3,2,1,0:T(8,128)S(1)} %shard_map.28) | data formatting | bytes 262144
Async XLA Ops:
  0.0 0.8 %copy-start = (f32[8,8,128]{2,1,0:T(8,128)S(1)}, f32[8,8,128]{2,1,0:T(8,128)}, u32[]{:S(2)}) copy-start(f32[8,8,128]{2,1,0:T(8,128)} %pot_hbm.1) | copy-start | bytes 98308

commit v5 on v4

--- a/solution.py
+++ b/solution.py
@@ -84,8 +84,6 @@
     load_x.start()
     load_y.start()
     load_pot.start()
-    load_x.wait()
-    load_y.wait()
     pl.semaphore_wait(barrier, 6)
 
     def halo(r, o):
@@ -94,22 +92,33 @@
         right_y = {"gy": peer("gy", 1)}
         left_y = {"gy": peer("gy", n_gy - 1)}
 
-        def move(buf, src, dst, send, recv, target):
+        def move(buf, src, dst, send, recv, target, source=None):
             return pltpu.make_async_remote_copy(
-                src_ref=buf.at[src], dst_ref=buf.at[dst], send_sem=send, recv_sem=recv,
+                src_ref=(buf if source is None else source).at[src], dst_ref=buf.at[dst], send_sem=send, recv_sem=recv,
                 device_id=target, device_id_type=MESH,
             )
 
-        every = slice(None)
+        whole = slice(None)
+        if r == 0:
+            return (
+                move(xb, (o, pl.ds(n_x - REACH, REACH)), (0, o, pl.ds(0, REACH)),
+                     x_send.at[0, 0], x_recv.at[0, 0, o], right_x, orb_ref),
+                move(xb, (o, pl.ds(0, REACH)), (0, o, pl.ds(n_x + REACH, REACH)),
+                     x_send.at[0, 1], x_recv.at[0, 1, o], left_x, orb_ref),
+                move(yb, (o,), (0, o, whole, pl.ds(0, n_y)),
+                     y_send.at[0, 0], y_recv.at[0, 0, o], right_y, orb_ref),
+                move(yb, (o,), (0, o, whole, pl.ds(2 * n_y, n_y)),
+                     y_send.at[0, 1], y_recv.at[0, 1, o], left_y, orb_ref),
+            )
         return (
             move(xb, (r, o, pl.ds(n_x, REACH)), (r, o, pl.ds(0, REACH)),
                  x_send.at[r, 0], x_recv.at[r, 0, o], right_x),
             move(xb, (r, o, pl.ds(REACH, REACH)), (r, o, pl.ds(n_x + REACH, REACH)),
                  x_send.at[r, 1], x_recv.at[r, 1, o], left_x),
-            move(yb, (r, o, every, pl.ds(2 * n_y - REACH, REACH)),
-                 (r, o, every, pl.ds(n_y - REACH, REACH)),
+            move(yb, (r, o, whole, pl.ds(2 * n_y - REACH, REACH)),
+                 (r, o, whole, pl.ds(n_y - REACH, REACH)),
                  y_send.at[r, 0], y_recv.at[r, 0, o], right_y),
-            move(yb, (r, o, every, pl.ds(n_y, REACH)), (r, o, every, pl.ds(2 * n_y, REACH)),
+            move(yb, (r, o, whole, pl.ds(n_y, REACH)), (r, o, whole, pl.ds(2 * n_y, REACH)),
                  y_send.at[r, 1], y_recv.at[r, 1, o], left_y),
         )
 
@@ -136,12 +145,36 @@
             result = result + (-0.5 * COEF[k] * scale) * pair
         return result
 
+    half = n_band // 2
+
+    def ring(direction, distance, source):
+        width = n_x // 2 if distance == half else n_x
+        block = every.at[source, pl.ds(direction * (n_x - width), width)]
+        return pltpu.make_async_remote_copy(
+            src_ref=block, dst_ref=block, send_sem=ring_send.at[direction, distance - 1],
+            recv_sem=ring_recv.at[direction, distance - 1],
+            device_id={"band": peer("band", n_band - 1 if direction else 1)},
+            device_id_type=MESH,
+        )
+
+    def source_at(direction, distance):
+        return peer("band", distance if direction else n_band - distance)
+
+    def pass_on(distance):
+        for direction in (0, 1):
+            source = source_at(direction, distance - 1)
+            if distance > 1:
+                ring(direction, distance - 1, source).wait_recv()
+            ring(direction, distance, source).start()
+
     @pl.loop(0, n_orb)
     def _(o):
         for copy in halo(0, o):
             copy.start()
 
     greet(near, "band", 1)
+    load_x.wait()
+    load_y.wait()
     load_pot.wait()
 
     @pl.loop(0, n_orb)
@@ -217,12 +250,17 @@
                 yb[r + 1, o, :, own_y] = result
                 for copy in halo(r + 1, o):
                     copy.start()
-                local_part(r + 1, o)
             else:
                 every[band, :, pl.ds(pl.multiple_of(o * n_y, n_y), n_y)] = result
                 for step in reversed(by_distance(n_band)):
                     spread(peer("band", step), o).start()
 
+        if r < 2:
+            @pl.loop(0, n_orb)
+            def _(o, r=r):
+                local_part(r + 1, o)
+
+    pass_on(1)
     if n_gx > 8:
         greet(far, "gx", 4)
     fc[rows_of(band)] = every[band, band]
@@ -260,41 +298,19 @@
             value = value + buf[step]
         return value
 
-    half = n_band // 2
-
-    def ring(direction, distance, source):
-        width = n_x // 2 if distance == half else n_x
-        block = every.at[source, pl.ds(direction * (n_x - width), width)]
-        return pltpu.make_async_remote_copy(
-            src_ref=block, dst_ref=block, send_sem=ring_send.at[direction, distance - 1],
-            recv_sem=ring_recv.at[direction, distance - 1],
-            device_id={"band": peer("band", n_band - 1 if direction else 1)},
-            device_id_type=MESH,
-        )
-
-    def source_at(direction, distance):
-        return peer("band", distance if direction else n_band - distance)
-
-    def pass_on(distance):
-        for direction in (0, 1):
-            source = source_at(direction, distance - 1)
-            if distance > 1:
-                ring(direction, distance - 1, source).wait_recv()
-            ring(direction, distance, source).start()
-
     first, second, third = phases
     sum_sends(*first[:2], packed, *first[2:])
-    pass_on(1)
+    pass_on(2)
     packed = sum_waits(*first[:2], packed, *first[2:])
     sum_sends(*second[:2], packed, *second[2:])
-    pass_on(2)
+    pass_on(3)
     packed = sum_waits(*second[:2], packed, *second[2:])
     if n_gx > 8:
         pl.semaphore_wait(far, 2)
     sum_sends(*third[:2], packed, *third[2:])
     for r in range(3):
         for buf, send in ((xb.at[r, :, pl.ds(0, REACH)], x_send),
-                          (yb.at[r, :, :, pl.ds(0, REACH)], y_send)):
+                          (yb.at[r, :, :, pl.ds(0, REACH if r else n_y)], y_send)):
             for direction in (0, 1):
                 pltpu.make_async_remote_copy(
                     src_ref=buf, dst_ref=buf, send_sem=send.at[r, direction],
@@ -306,7 +322,7 @@
     for steps, where, buf, send, recv in phases[:2]:
         for step in steps:
             share(step, where, buf, send, recv).wait_send()
-    for distance in range(3, half + 1):
+    for distance in range(4, half + 1):
         pass_on(distance)
     packed = sum_waits(*third[:2], packed, *third[2:])
     cells_all = float(n_x * n_y * n_z * n_gx * n_gy)
@@ -397,12 +413,15 @@
             *[pltpu.SemaphoreType.REGULAR] * 3,
         ],
         compiler_params=pltpu.CompilerParams(
-            collective_id=0, has_side_effects=True, vmem_limit_bytes=55008 * 1024
+            collective_id=0, has_side_effects=True, vmem_limit_bytes=32 * 1024 * 1024
         ),
         cost_estimate=pl.CostEstimate(
             flops=16_000_000, bytes_accessed=4 * 2 * orbitals.size, transcendentals=0
         ),
-    )(orbitals, potential)
+    )(
+        pltpu.with_memory_space_constraint(orbitals, pltpu.HBM),
+        pltpu.with_memory_space_constraint(potential, pltpu.HBM),
+    )
 
 
 def solution(mesh):

time: 57.3 us -> 54.5 us (0.951)
  the two profiles are of different devices: /device:TPU:2 before, /device:TPU:1 now
where the time goes in v5:
time: 54.5 us; the launch traced here: 53.7 us
  Pallas kernels  53 us (97%)
  local copies, waits for them, and re-layouts  0.66 us (1%)
    pallas_call x1, Pallas kernels, local(): pl.pallas_call(functools.partial(kernel, sizes), out_shape=jax.ShapeDtype...  53 us

profile of v5, /device:TPU:1, one launch (start us, length us, event | category | flops | bytes accessed | tf_op | source)
XLA Modules:
  0.0 53.7 jit_solution(10296579449842315780)
XLA Ops:
  0.0 53.0 %shard_map.28 = f32[4,8,8,128]{3,2,1,0:T(8,128)S(1)} custom-call(f32[4,8,8,128]{3,2,1,0:T(8,128)} %orb_ref.1, f32[8,8,128]{2,1,0:T(8,128)} %pot_hbm.1), custom_call_target="tpu_custom_call" | custom-call | flops 16000000 | bytes 262144 | tf_op jit(solution)/shard_map/pallas_call | solution.py:392
  53.1 0.7 %copy.4 = f32[4,8,8,128]{3,2,1,0:T(8,128)} copy(f32[4,8,8,128]{3,2,1,0:T(8,128)S(1)} %shard_map.28) | data formatting | bytes 262144

commit v6 on v5

--- a/solution.py
+++ b/solution.py
@@ -39,12 +39,9 @@
 CENTRE, ROUNDS = chebyshev_weights()
 
 
-def split_three(value):
+def split_two(value):
     high = value.astype(jnp.bfloat16)
-    rest = value - high.astype(jnp.float32)
-    middle = rest.astype(jnp.bfloat16)
-    low = (rest - middle.astype(jnp.float32)).astype(jnp.bfloat16)
-    return high, middle, low
+    return high, (value - high.astype(jnp.float32)).astype(jnp.bfloat16)
 
 
 def kernel(
@@ -62,15 +59,23 @@
     me = {"gx": gx, "gy": gy, "band": band}
     counts = {"gx": n_gx, "gy": n_gy, "band": n_band}
 
+    ring_of = {
+        axis: [lax.rem(me[axis] + step, counts[axis]) for step in range(counts[axis])]
+        for axis in ("gx", "gy", "band")
+    }
+
     def peer(axis, step):
-        return lax.rem(me[axis] + step, counts[axis])
+        return ring_of[axis][step % counts[axis]]
+
+    def device(**where):
+        return tuple(where.get(axis, me[axis]) for axis in ("gx", "gy", "band"))
 
     barrier = pltpu.get_barrier_semaphore()
 
     def greet(semaphore, axis, distance):
         for step in (distance, counts[axis] - distance):
             pl.semaphore_signal(
-                semaphore, inc=1, device_id={axis: peer(axis, step)}, device_id_type=MESH
+                semaphore, inc=1, device_id=device(**{axis: peer(axis, step)}), device_id_type=MESH
             )
 
     for axis in ("gx", "gy", "band"):
@@ -95,7 +100,7 @@
         def move(buf, src, dst, send, recv, target, source=None):
             return pltpu.make_async_remote_copy(
                 src_ref=(buf if source is None else source).at[src], dst_ref=buf.at[dst], send_sem=send, recv_sem=recv,
-                device_id=target, device_id_type=MESH,
+                device_id=device(**target), device_id_type=MESH,
             )
 
         whole = slice(None)
@@ -153,7 +158,7 @@
         return pltpu.make_async_remote_copy(
             src_ref=block, dst_ref=block, send_sem=ring_send.at[direction, distance - 1],
             recv_sem=ring_recv.at[direction, distance - 1],
-            device_id={"band": peer("band", n_band - 1 if direction else 1)},
+            device_id=device(band=peer("band", n_band - 1 if direction else 1)),
             device_id_type=MESH,
         )
 
@@ -192,21 +197,29 @@
             src_ref=every.at[band, target, pl.ds(start, n_y)],
             dst_ref=fc.at[pl.ds(pl.multiple_of(depth * band + start, n_y), n_y)],
             send_sem=a_send.at[target], recv_sem=a_recv.at[band],
-            device_id={"band": target}, device_id_type=MESH,
+            device_id=device(band=target), device_id_type=MESH,
         )
 
     def spread_whole(source, target):
         return pltpu.make_async_remote_copy(
             src_ref=every.at[band, target], dst_ref=fc.at[rows_of(source)],
             send_sem=a_send.at[target], recv_sem=a_recv.at[source],
-            device_id={"band": target}, device_id_type=MESH,
+            device_id=device(band=target), device_id_type=MESH,
         )
 
     def share(step, where, buf, send, recv):
         return pltpu.make_async_remote_copy(
-            src_ref=buf.at[0], dst_ref=buf.at[step], send_sem=send.at[step],
-            recv_sem=recv.at[step], device_id=where(step), device_id_type=MESH,
+            src_ref=buf.at[0], dst_ref=buf.at[step], send_sem=send.at[0],
+            recv_sem=recv.at[step], device_id=device(**where(step)), device_id_type=MESH,
         )
+
+    def sum_sent(steps, where, buf, send, recv):
+        if steps:
+            sent = buf.at[pl.ds(1, len(steps))]
+            pltpu.make_async_remote_copy(
+                src_ref=sent, dst_ref=sent, send_sem=send.at[0], recv_sem=recv.at[1],
+                device_id=device(**where(steps[0])), device_id_type=MESH,
+            ).wait_send()
 
     def by_distance(count):
         return sorted(range(1, count), key=lambda step: min(step, count - step))
@@ -269,16 +282,16 @@
 
     parts = []
     for y in range(n_y):
-        parts.append(split_three(fc[pl.ds(y, total, stride=n_y), :]))
+        parts.append(split_two(fc[pl.ds(y, total, stride=n_y), :]))
     stacked = jnp.concatenate([jnp.concatenate(part, axis=0) for part in parts], axis=1)
     blocks = lax.dot_general(
         stacked, stacked, (((1,), (1,)), ((), ())), preferred_element_type=jnp.float32
     )
-    blocks = blocks[:total] + blocks[total : 2 * total] + blocks[2 * total :]
-    gram[:, : 3 * total] = blocks
-    gram[:, 3 * total :] = jnp.zeros((total, n_z - 3 * total), jnp.float32)
+    blocks = blocks[:total] + blocks[total:]
+    gram[:, : 2 * total] = blocks
+    gram[:, 2 * total :] = jnp.zeros((total, n_z - 2 * total), jnp.float32)
     wide = gram[...]
-    wide = wide + pltpu.roll(wide, n_z - total, 1) + pltpu.roll(wide, n_z - 2 * total, 1)
+    wide = wide + pltpu.roll(wide, n_z - total, 1)
     lane = lax.broadcasted_iota(jnp.int32, (8, n_z), 1)
     row = lax.broadcasted_iota(jnp.int32, (8, n_z), 0)
     groups = total // 8
@@ -314,16 +327,18 @@
             for direction in (0, 1):
                 pltpu.make_async_remote_copy(
                     src_ref=buf, dst_ref=buf, send_sem=send.at[r, direction],
-                    recv_sem=x_recv.at[0, 0, 0], device_id={"gx": peer("gx", 1)},
+                    recv_sem=x_recv.at[0, 0, 0], device_id=device(gx=peer("gx", 1)),
                     device_id_type=MESH,
                 ).wait_send()
     for step in by_distance(n_band):
         spread_whole(band, peer("band", step)).wait_send()
-    for steps, where, buf, send, recv in phases[:2]:
-        for step in steps:
-            share(step, where, buf, send, recv).wait_send()
+    sum_sent(*first)
+    sum_sent(*second)
     for distance in range(4, half + 1):
         pass_on(distance)
+    for direction in (0, 1):
+        for distance in (1, 2):
+            ring(direction, distance, source_at(direction, distance - 1)).wait_send()
     packed = sum_waits(*third[:2], packed, *third[2:])
     cells_all = float(n_x * n_y * n_z * n_gx * n_gy)
     packed = packed * (1.0 / cells_all)
@@ -375,10 +390,9 @@
     for i in range(n_orb):
         for x in range(n_x):
             out_ref[i, x] = results[i][x]
-    for step in third[0]:
-        share(step, *third[1:]).wait_send()
+    sum_sent(*third)
     for direction in (0, 1):
-        for distance in range(1, half + 1):
+        for distance in range(3, half + 1):
             ring(direction, distance, source_at(direction, distance - 1)).wait_send()
 
 

time: 54.5 us -> 54.5 us (level); the launches traced: 53.7 us -> 54.3 us
  Pallas kernels: 53 us -> 53.6 us
    pallas_call x1, Pallas kernels: 53 us -> 53.6 us  [local(): pl.pallas_call(functools.partial(kernel, sizes), out_shape=jax.ShapeDtype...]
where the time goes in v6:
time: 54.5 us; the launch traced here: 54.3 us
  Pallas kernels  53.6 us (98%)
  local copies, waits for them, and re-layouts  0.66 us (1%)
    pallas_call x1, Pallas kernels, local(): pl.pallas_call(functools.partial(kernel, sizes), out_shape=jax.ShapeDtype...  53.6 us

profile of v6, /device:TPU:1, one launch (start us, length us, event | category | flops | bytes accessed | tf_op | source)
XLA Modules:
  0.0 54.3 jit_solution(14870547073307924524)
XLA Ops:
  0.0 53.6 %shard_map.28 = f32[4,8,8,128]{3,2,1,0:T(8,128)S(1)} custom-call(f32[4,8,8,128]{3,2,1,0:T(8,128)} %orb_ref.1, f32[8,8,128]{2,1,0:T(8,128)} %pot_hbm.1), custom_call_target="tpu_custom_call" | custom-call | flops 16000000 | bytes 262144 | tf_op jit(solution)/shard_map/pallas_call | solution.py:406
  53.6 0.7 %copy.4 = f32[4,8,8,128]{3,2,1,0:T(8,128)} copy(f32[4,8,8,128]{3,2,1,0:T(8,128)S(1)} %shard_map.28) | data formatting | bytes 262144

commit v7 on v6

--- a/solution.py
+++ b/solution.py
@@ -311,16 +311,11 @@
             value = value + buf[step]
         return value
 
-    first, second, third = phases
+    second, third, first = phases
+    if n_gx > 8:
+        pl.semaphore_wait(far, 2)
     sum_sends(*first[:2], packed, *first[2:])
     pass_on(2)
-    packed = sum_waits(*first[:2], packed, *first[2:])
-    sum_sends(*second[:2], packed, *second[2:])
-    pass_on(3)
-    packed = sum_waits(*second[:2], packed, *second[2:])
-    if n_gx > 8:
-        pl.semaphore_wait(far, 2)
-    sum_sends(*third[:2], packed, *third[2:])
     for r in range(3):
         for buf, send in ((xb.at[r, :, pl.ds(0, REACH)], x_send),
                           (yb.at[r, :, :, pl.ds(0, REACH if r else n_y)], y_send)):
@@ -332,13 +327,18 @@
                 ).wait_send()
     for step in by_distance(n_band):
         spread_whole(band, peer("band", step)).wait_send()
+    for distance in range(3, half):
+        pass_on(distance)
+    packed = sum_waits(*first[:2], packed, *first[2:])
+    sum_sends(*second[:2], packed, *second[2:])
+    pass_on(half)
     sum_sent(*first)
-    sum_sent(*second)
-    for distance in range(4, half + 1):
-        pass_on(distance)
     for direction in (0, 1):
         for distance in (1, 2):
             ring(direction, distance, source_at(direction, distance - 1)).wait_send()
+    packed = sum_waits(*second[:2], packed, *second[2:])
+    sum_sends(*third[:2], packed, *third[2:])
+    sum_sent(*second)
     packed = sum_waits(*third[:2], packed, *third[2:])
     cells_all = float(n_x * n_y * n_z * n_gx * n_gy)
     packed = packed * (1.0 / cells_all)

time: 54.5 us -> 57.9 us (1.062)
  Pallas kernels: 53.6 us -> 57.1 us
    pallas_call x1, Pallas kernels: 53.6 us -> 57.1 us  [local(): pl.pallas_call(functools.partial(kernel, sizes), out_shape=jax.ShapeDtype...]
where the time goes in v7:
time: 57.9 us; the launch traced here: 57.8 us
  Pallas kernels  57.1 us (99%)
  local copies, waits for them, and re-layouts  0.66 us (1%)
    pallas_call x1, Pallas kernels, local(): pl.pallas_call(functools.partial(kernel, sizes), out_shape=jax.ShapeDtype...  57.1 us

profile of v7, /device:TPU:1, one launch (start us, length us, event | category | flops | bytes accessed | tf_op | source)
XLA Modules:
  0.0 57.8 jit_solution(363194502286115547)
XLA Ops:
  0.0 57.1 %shard_map.28 = f32[4,8,8,128]{3,2,1,0:T(8,128)S(1)} custom-call(f32[4,8,8,128]{3,2,1,0:T(8,128)} %orb_ref.1, f32[8,8,128]{2,1,0:T(8,128)} %pot_hbm.1), custom_call_target="tpu_custom_call" | custom-call | flops 16000000 | bytes 262144 | tf_op jit(solution)/shard_map/pallas_call | solution.py:406
  57.1 0.7 %copy.4 = f32[4,8,8,128]{3,2,1,0:T(8,128)} copy(f32[4,8,8,128]{3,2,1,0:T(8,128)S(1)} %shard_map.28) | data formatting | bytes 262144
